TPU v7x, 256 devices: a whole 4x4x8 slice. The times are simulated.
256 devices in a mesh: grp: 8 (over x, y_hi), blk: 32 (over z, y_lo, core).
Axes of the slice: x: 4, y: 4 (y_hi: 2, y_lo: 2; y = y_hi * 2 + y_lo), z: 8, core: 2. Of those that a mesh axis runs over, the one named last changes fastest.
Arguments:
- image_embed: float32 [262144, 768], P(('grp', 'blk')), may hold values from -0.2 to 0.2
- caption_embed: float32 [262144, 768], P(('grp', 'blk')), may hold values from -0.2 to 0.2
- pair_ids: int32 [262144], P(('grp', 'blk')), may hold values from 0 to 262143, as said below
- log_scale: float32 [1], replicated, may hold values from 1 to 2
- logit_bias: float32 [1], replicated, may hold values from -3 to -0.5
Outputs:
- image_grad: float32 [262144, 768], P(('grp', 'blk'))
- caption_grad: float32 [262144, 768], P(('grp', 'blk'))
Inputs may be any that keep to these rules, and one draw needn't show every extreme that they name: `pair_ids`: the ids of the rows of each block of 1024 rows are a permutation of that block's own row indices.
All inputs are finite; a program needn't handle non-finite values.
Results may differ from a plain program's by a relative error of at most 0.0003.
Values sent between devices are 32-bit elements; how exact they have to be, the bound alone decides.
No kernel may reach another device: no remote copies, remote signals or barrier semaphores. Data moves between devices by JAX's collectives and lax.ppermute only.
A program may use at most 128 MiB of HBM per device.

v0:
```python
import functools

import jax
import jax.numpy as jnp
from jax import lax
from jax.experimental import pallas as pl
from jax.experimental.pallas import tpu as pltpu
from jax.sharding import PartitionSpec as P

EPS = 1e-06
TILE = 256
VMEM = 42
CUTS = (128, 384)
SCALE = dict(own=1.0, part_a=1.0, cyc_captions=1.0, part_b=3.0, rest=2.0)
BACK = (768, 960)
NT = (((1,), (1,)), ((), ()))
NN = (((1,), (0,)), ((), ()))
TN = (((0,), (0,)), ((), ()))
F32 = jnp.float32
SMEM = pl.BlockSpec(memory_space=pltpu.SMEM)
PARAMS = pltpu.CompilerParams(vmem_limit_bytes=VMEM * 1024 * 1024)
SMALL = pltpu.CompilerParams(vmem_limit_bytes=12 * 1024 * 1024)


def passed_along(block, axis, distance):
    n = lax.axis_size(axis)
    return lax.ppermute(block, axis, [((i - distance) % n, i) for i in range(n)])


def partner(block, axis):
    n = lax.axis_size(axis)
    return lax.ppermute(block, axis, [(i, (i + n // 2) % n) for i in range(n)])


def split(x):
    hi = x.astype(jnp.bfloat16)
    lo = (x - hi.astype(F32)).astype(jnp.bfloat16)
    return hi, lo


def product(a, b, dims):
    dot = functools.partial(lax.dot_general, dimension_numbers=dims, preferred_element_type=F32)
    return dot(a[0], b[0]) + (dot(a[0], b[1]) + dot(a[1], b[0]))


def norm_of(x):
    return jnp.sqrt(jnp.sum(x * x, axis=-1, keepdims=True) + EPS)


def unit(x):
    return x * (1.0 / norm_of(x))


def projected(raw, grad):
    r = 1.0 / norm_of(raw)
    one = raw * r
    return (grad - one * jnp.sum(one * grad, axis=-1, keepdims=True)) * r


def weights(u, v, scal_ref, labels=None):
    weight = jax.nn.sigmoid(scal_ref[0] * product(v, u, NT) + scal_ref[1])
    if labels is not None:
        weight = weight - labels
    return split(scal_ref[0] * weight)


def own_kernel(first_ref, scal_ref, ids_ref, image_ref, caption_ref, after_ref, u_ref, hi_ref, lo_ref, du_ref, dv_ref):
    del after_ref
    t = pl.program_id(0)
    tile = caption_ref.shape[0]

    @pl.when(t == 0)
    def _():
        u = unit(image_ref[...])
        u_ref[...] = u
        hi_ref[...], lo_ref[...] = split(u)
        du_ref[...] = jnp.zeros_like(du_ref)

    columns = first_ref[0] + t * tile + lax.broadcasted_iota(jnp.int32, (tile, ids_ref.shape[1]), 0)
    labels = (ids_ref[...] == columns).astype(F32)
    u = (hi_ref[...], lo_ref[...])
    v = split(unit(caption_ref[...]))
    g = weights(u, v, scal_ref, labels)
    dv_ref[...] = product(g, u, NN)
    du_ref[...] += product(g, v, TN)


def score_kernel(chunks, passed, tile, scal_ref, hi_ref, lo_ref, *rest):
    caption_refs, du_in_ref, du_ref = rest[:chunks], rest[chunks], rest[chunks + 1 + passed]
    dv_refs, (v_hi_ref, v_lo_ref) = rest[chunks + 2 + 2 * passed : -2], rest[-2:]
    t = pl.program_id(0)

    @pl.when(t == 0)
    def _():
        at = 0
        for ref in caption_refs:
            n = ref.shape[0]
            v_hi_ref[at : at + n, :], v_lo_ref[at : at + n, :] = split(unit(ref[...]))
            at += n
        du_ref[...] = du_in_ref[...]

    rows = pl.ds(pl.multiple_of(t * tile, 16), tile)
    u = (hi_ref[...], lo_ref[...])
    v = (v_hi_ref[rows, :], v_lo_ref[rows, :])
    g = weights(u, v, scal_ref)
    if dv_refs:
        dv = product(g, u, NN)
        for step in range(v_hi_ref.shape[0] // tile):

            @pl.when(t == step)
            def _():
                at = 0
                for ref in dv_refs:
                    a, b = max(at, step * tile), min(at + ref.shape[0], (step + 1) * tile)
                    if a < b:
                        ref[a - at : b - at, :] = dv[a - step * tile : b - step * tile, :]
                    at += ref.shape[0]

    du_ref[...] += product(g, v, TN)


def returns_kernel(tile, scal_ref, hi_ref, lo_ref, caption_ref, after_ref, g_hi_ref, g_lo_ref, v_hi_ref, v_lo_ref, *dv_refs):
    del after_ref
    t = pl.program_id(0)
    u = (hi_ref[...], lo_ref[...])
    v = split(unit(caption_ref[...]))
    v_hi_ref[...], v_lo_ref[...] = v
    g = weights(u, v, scal_ref)
    g_hi_ref[...], g_lo_ref[...] = g
    dv = product(g, u, NN)
    for step in range(sum(ref.shape[0] for ref in dv_refs) // tile):

        @pl.when(t == step)
        def _():
            at = 0
            for ref in dv_refs:
                a, b = max(at, step * tile), min(at + ref.shape[0], (step + 1) * tile)
                if a < b:
                    ref[a - at : b - at, :] = dv[a - step * tile : b - step * tile, :]
                at += ref.shape[0]


def rest_kernel(g_hi_ref, g_lo_ref, v_hi_ref, v_lo_ref, du_ref, image_ref, grad_ref):
    du = du_ref[...] + product((g_hi_ref[...], g_lo_ref[...]), (v_hi_ref[...], v_lo_ref[...]), TN)
    grad_ref[...] = projected(image_ref[...], du)


def images_kernel(scal_ref, u_ref, caption_ref, dv_in_ref, dv_ref, hi_ref, lo_ref):
    @pl.when(pl.program_id(0) == 0)
    def _():
        hi_ref[...], lo_ref[...] = split(u_ref[...])

    u = (hi_ref[...], lo_ref[...])
    g = weights(u, split(unit(caption_ref[...])), scal_ref)
    dv_ref[...] = dv_in_ref[...] + product(g, u, NN)


def finish_kernel(caption_ref, base_ref, part_ref, *rest):
    rest[-1][...] = projected(caption_ref[...], base_ref[...] + part_ref[...])


def whole(shape):
    return pl.BlockSpec(shape, lambda t: (0,) * len(shape), pipeline_mode=pl.Buffered(1))


def result(shape):
    return pl.BlockSpec(shape, lambda t: (0,) * len(shape))


def blocks(tile, d, first=0):
    return pl.BlockSpec((tile, d), lambda t: (t + first, 0))


def shape(rows, d, dtype=F32):
    return jax.ShapeDtypeStruct((rows, d), dtype)


def halves(rows, d):
    return [pltpu.VMEM((rows, d), jnp.bfloat16)] * 2


def cost(products, rows, cols, d, scale=1.0):
    return pl.CostEstimate(flops=int(scale * 2 * 3 * products * rows * cols * d), bytes_accessed=16 * rows * d, transcendentals=rows * cols)


def own_block(first, scal, ids, image, caption, after):
    rows, d = image.shape
    return pl.pallas_call(
        own_kernel,
        grid=(rows // TILE,),
        in_specs=[SMEM, SMEM, whole((1, rows)), whole((rows, d)), blocks(TILE, d), pl.BlockSpec(memory_space=pl.ANY)],
        out_specs=[result((rows, d))] * 4 + [blocks(TILE, d)],
        out_shape=[shape(rows, d)] + [shape(rows, d, jnp.bfloat16)] * 2 + [shape(rows, d)] * 2,
        compiler_params=PARAMS,
        cost_estimate=cost(3, rows, rows, d, SCALE['own']),
        name="own",
    )(first, scal, ids, image, caption, after)


def score(scal, u, chunks, du, pieces, name, passed=None):
    rows, d = du.shape
    part = sum(c.shape[0] for c in chunks)
    tile = max(c for c in range(16, TILE + 128, 16) if part % c == 0)
    extra = [] if passed is None else [passed]
    kept = [pl.BlockSpec(memory_space=pl.ANY)] * len(extra)
    return pl.pallas_call(
        functools.partial(score_kernel, len(chunks), len(extra), tile),
        grid=(part // tile,),
        in_specs=[SMEM] + [whole((rows, d))] * 2 + [whole(c.shape) for c in chunks] + [whole((rows, d))] + kept,
        out_specs=[result((rows, d))] + kept + [result((n, d)) for n in pieces],
        out_shape=[shape(rows, d)] + [shape(*x.shape) for x in extra] + [shape(n, d) for n in pieces],
        scratch_shapes=halves(part, d),
        input_output_aliases={4 + len(chunks): 1} if extra else {},
        compiler_params=PARAMS,
        cost_estimate=cost(3 if pieces else 2, part, rows, d, SCALE[name]),
        name=name,
    )(scal, *u, *chunks, du, *extra)


def cycle_images(scal, u, caption, dv):
    rows, d = dv.shape
    return pl.pallas_call(
        images_kernel,
        grid=(rows // TILE,),
        in_specs=[SMEM, whole((rows, d)), blocks(TILE, d), blocks(TILE, d)],
        out_specs=blocks(TILE, d),
        out_shape=shape(rows, d),
        scratch_shapes=halves(rows, d),
        compiler_params=PARAMS,
        cost_estimate=cost(2, rows, rows, d),
        name="cyc_images",
    )(scal, u, caption, dv)


def returns(scal, u, captions, pieces, after):
    rows, d = u[0].shape
    part = captions.shape[0]
    tile = max(c for c in range(16, TILE + 128, 16) if part % c == 0)
    out = [(part, rows)] * 2 + [(part, d)] * 2
    return pl.pallas_call(
        functools.partial(returns_kernel, tile),
        grid=(part // tile,),
        in_specs=[SMEM] + [whole((rows, d))] * 2 + [blocks(tile, d), pl.BlockSpec(memory_space=pl.ANY)],
        out_specs=[blocks(tile, c) for _, c in out] + [result((n, d)) for n in pieces],
        out_shape=[shape(n, c, jnp.bfloat16) for n, c in out] + [shape(n, d) for n in pieces],
        compiler_params=PARAMS,
        cost_estimate=cost(2, part, rows, d, SCALE["part_b"]),
        name="part_b",
    )(scal, *u, captions, after)


def image_gradient(g, v, du, image):
    rows, d = du.shape
    part = v[0].shape[0]
    return pl.pallas_call(
        rest_kernel,
        grid=(rows // TILE,),
        in_specs=[pl.BlockSpec((part, TILE), lambda t: (0, t))] * 2 + [whole((part, d))] * 2 + [blocks(TILE, d)] * 2,
        out_specs=blocks(TILE, d),
        out_shape=shape(rows, d),
        compiler_params=PARAMS,
        cost_estimate=cost(1, part, rows, d, SCALE["rest"]),
        name="image_grad",
    )(*g, *v, du, image)


def finish(caption, base, part, at, grad=None):
    rows, d = caption.shape
    n = part.shape[0]
    tile = max(c for c in range(8, 200, 8) if n % c == 0 and at % c == 0)
    more = grad is not None
    return pl.pallas_call(
        finish_kernel,
        grid=(n // tile,),
        in_specs=[blocks(tile, d, at // tile)] * 2 + [blocks(tile, d)] + [pl.BlockSpec(memory_space=pl.ANY)] * more,
        out_specs=blocks(tile, d, at // tile),
        out_shape=shape(rows, d),
        input_output_aliases={3: 0} if more else {},
        compiler_params=SMALL,
        cost_estimate=pl.CostEstimate(flops=10 * part.size, bytes_accessed=16 * part.size, transcendentals=0),
        name="finish",
    )(caption, base, part, *([grad] if more else []))


def body(image_embed, caption_embed, pair_ids, log_scale, logit_bias):
    rows = image_embed.shape[0]
    chunks, later = [], caption_embed
    for a, b in zip((0,) + CUTS, CUTS + (rows,)):
        chunk, later = lax.optimization_barrier((later[a:b], later))
        chunks.append(chunk)
    parts = [partner(c, "grp") for c in chunks]
    cycles = [passed_along(c, "blk", 1) for c in chunks]
    scal = jnp.concatenate([jnp.exp(log_scale), logit_bias])
    first = (lax.axis_index("grp") * lax.axis_size("blk") + lax.axis_index("blk")) * rows
    one, hi, lo, du, dv = own_block(first.astype(jnp.int32)[None], scal, pair_ids[None, :], image_embed, caption_embed, parts[0])
    u = (hi, lo)
    du, one, dv_part0 = score(scal, u, parts[:-1], du, [CUTS[-1]], "part_a", one)
    back0 = partner(dv_part0, "grp")
    next_u = passed_along(one, "blk", -1)
    (du,) = score(scal, u, cycles, du, [], "cyc_captions")
    edges = CUTS[-1:] + BACK + (rows,)
    pieces = [b - a for a, b in zip(edges, edges[1:])]
    g_hi, g_lo, v_hi, v_lo, *dv_part1 = returns(scal, u, parts[-1], pieces, du)
    backs = [partner(piece, "grp") for piece in dv_part1]
    base = cycle_images(scal, next_u, caption_embed, dv)
    image_grad = image_gradient((g_hi, g_lo), (v_hi, v_lo), du, image_embed)
    grad = finish(caption_embed, base, back0, 0)
    for at, back in zip(edges, backs):
        grad = finish(caption_embed, base, back, at, grad)
    return (image_grad, grad)


def solution(mesh):
    in_specs = (P(("grp", "blk"), None), P(("grp", "blk"), None), P(("grp", "blk")), P(), P())
    out_specs = (P(("grp", "blk"), None), P(("grp", "blk"), None))
    return jax.shard_map(body, mesh=mesh, in_specs=in_specs, out_specs=out_specs, check_vma=False)
```

profile of v0, /device:TPU:130, one launch (start us, length us, event | category | flops | bytes accessed | tf_op | source)
XLA Modules:
  0.0 142.3 jit_solution(6437079625508837621)
XLA Ops:
  0.6 0.0 copy-start.6
  0.6 1.8 %slice.9 = f32[128,768]{1,0:T(8,128)} slice(f32[1024,768]{1,0:T(8,128)} %caption_ref.11), slice={[0:128], [0:768]} | slice | bytes 786432 | tf_op jit(solution)/shard_map/slice | solution.py:289
  2.4 2.1 %collective-permute-start = (f32[128,768]{1,0:T(8,128)}, f32[128,768]{1,0:T(8,128)S(1)}, u32[]{:S(2)}, u32[]{:S(2)}) collective-permute-start(f32[128,768]{1,0:T(8,128)} %slice.9), channel_id=1, source_target_pairs={{0,128},{32,160},{64,192},{96,224},{128,0},{160,32},{192,64},{224,... | collective-permute-start | bytes 1179656 | tf_op jit(solution)/shard_map/ppermute | solution.py:32
  4.6 2.2 %slice.10 = f32[256,768]{1,0:T(8,128)} slice(f32[1024,768]{1,0:T(8,128)} %caption_ref.11), slice={[128:384], [0:768]} | slice | bytes 1572864 | tf_op jit(solution)/shard_map/slice | solution.py:289
  6.7 1.4 collective-permute-start.5
  8.1 0.0 collective-permute-start.3
  8.1 1.7 %collective-permute-start.2 = (f32[128,768]{1,0:T(8,128)}, f32[128,768]{1,0:T(8,128)S(1)}, u32[]{:S(2)}, u32[]{:S(2)}) collective-permute-start(f32[128,768]{1,0:T(8,128)} %slice.9), channel_id=1, source_target_pairs={{31,0},{0,1},{1,2},{2,3},{3,4},{4,5},{5,6},{6,7},{7,8},{8,9},{9,10... | collective-permute-start | bytes 1179656 | tf_op jit(solution)/shard_map/ppermute | solution.py:27
  9.8 3.0 %slice.11 = f32[640,768]{1,0:T(8,128)} slice(f32[1024,768]{1,0:T(8,128)} %caption_ref.11), slice={[384:1024], [0:768]} | slice | bytes 3932160 | tf_op jit(solution)/shard_map/slice | solution.py:289
  12.8 0.0 collective-permute-start.4
  14.2 0.1 pad_maximum_fusion.scal_ref
  14.2 1.9 %collective-permute-done.after_ref.rest_0_ = f32[128,768]{1,0:T(8,128)S(1)} collective-permute-done((f32[128,768]{1,0:T(8,128)}, f32[128,768]{1,0:T(8,128)S(1)}, u32[]{:S(2)}, u32[]{:S(2)}) %collective-permute-start) | collective-permute-done | bytes 393248 | tf_op jit(solution)/shard_map/ppermute | solution.py:32
  16.1 0.0 copy-start.4
  16.1 2.1 %collective-permute-start.1 = (f32[640,768]{1,0:T(8,128)}, f32[640,768]{1,0:T(8,128)S(1)}, u32[]{:S(2)}, u32[]{:S(2)}) collective-permute-start(f32[640,768]{1,0:T(8,128)} %slice.11), channel_id=1, source_target_pairs={{0,128},{32,160},{64,192},{96,224},{128,0},{160,32},{192,64},{224,... | collective-permute-start | bytes 5898248 | tf_op jit(solution)/shard_map/ppermute | solution.py:32
  18.3 0.0 copy-done.6
  18.3 19.9 %own.1 = (f32[1024,768]{1,0:T(8,128)}, bf16[1024,768]{1,0:T(8,128)(2,1)S(1)}, bf16[1024,768]{1,0:T(8,128)(2,1)S(1)}, f32[1024,768]{1,0:T(8,128)S(1)}, f32[1024,768]{1,0:T(8,128)}) custom-call(s32[1]{0:T(128)} %bitcast.first_ref, f32[2]{0:T(128)S(1)} %pad_maximum_fusion.scal_ref, s32[1,1024]{1,0:T(1,128)S(1)} %bitcast.2, f32[1024,768]{1,0:T(8,128)} %image_ref.3, ...), custom_call_target="tpu_custom_call" | custom-call | flops 14495514624 | bytes 12582912 | tf_op jit(solution)/shard_map/own/pallas_call | solution.py:188
  38.2 0.0 copy-done.4
  38.2 0.0 copy-start.10
  38.2 1.7 %copy-done.10 = f32[1024,768]{1,0:T(8,128)} copy-done((f32[1024,768]{1,0:T(8,128)}, f32[1024,768]{1,0:T(8,128)S(1)}, u32[]{:S(2)}) %copy-start.10) | copy-done | bytes 3145752
  39.9 0.0 collective-permute-done.5.rest_1_
  39.9 0.0 copy-start.2
  39.9 0.9 copy-done.2
  40.8 0.0 copy-start.3
  40.8 1.1 copy-done.3
  41.9 0.0 copy-start.5
  41.9 1.0 copy-done.5
  42.9 12.0 %part_a.1 = (f32[1024,768]{1,0:T(8,128)S(1)}, f32[1024,768]{1,0:T(8,128)}, f32[384,768]{1,0:T(8,128)S(1)}) custom-call(f32[2]{0:T(128)S(1)} %pad_maximum_fusion.scal_ref, bf16[1024,768]{1,0:T(8,128)(2,1)S(1)} %get-tuple-element.23.hi_ref, bf16[1024,768]{1,0:T(8,128)(2,1)S(1)} %get-tuple-element.24.lo_ref, ...), custom_call_target="tpu_custom_call", output_to_operand_aliasing={{1}: (6, {})} | custom-call | flops 5435817984 | bytes 4718592 | tf_op jit(solution)/shard_map/part_a/pallas_call | solution.py:206
  54.9 0.0 copy-start.9
  55.0 1.7 %copy-done.9 = f32[1024,768]{1,0:T(8,128)} copy-done((f32[1024,768]{1,0:T(8,128)}, f32[1024,768]{1,0:T(8,128)S(1)}, u32[]{:S(2)}) %copy-start.9) | copy-done | bytes 3145752
  56.6 1.9 %collective-permute-start.6 = (f32[1024,768]{1,0:T(8,128)}, f32[1024,768]{1,0:T(8,128)}, u32[]{:S(2)}, u32[]{:S(2)}) collective-permute-start(f32[1024,768]{1,0:T(8,128)} %get-tuple-element.36), channel_id=1, source_target_pairs={{1,0},{2,1},{3,2},{4,3},{5,4},{6,5},{7,6},{8,7},{9,8},{10,9},{11,1... | collective-permute-start | bytes 9437192 | tf_op jit(solution)/shard_map/ppermute | solution.py:27
  58.5 0.0 collective-permute-done.2.rest_0_
  58.5 1.4 collective-permute-start.10
  59.9 0.0 collective-permute-done.3.rest_1_
  59.9 0.0 collective-permute-done.4.rest_2_
  59.9 14.5 %cyc_captions.1.after_ref.du_ref = f32[1024,768]{1,0:T(8,128)S(1)} custom-call(f32[2]{0:T(128)S(1)} %pad_maximum_fusion.scal_ref, bf16[1024,768]{1,0:T(8,128)(2,1)S(1)} %get-tuple-element.23.hi_ref, bf16[1024,768]{1,0:T(8,128)(2,1)S(1)} %get-tuple-element.24.lo_ref, f32[128,768]{1,0:T(8,128)S(1)} %collective-permute-done.2.rest_0_, ...), custom_call_target="tpu_custom_call" | custom-call | flops 9663676416 | bytes 12582912 | tf_op jit(solution)/shard_map/cyc_captions/pallas_call | solution.py:206
  74.5 0.0 copy-start.7
  74.5 1.7 %copy-done.7 = f32[1024,768]{1,0:T(8,128)} copy-done((f32[1024,768]{1,0:T(8,128)}, f32[1024,768]{1,0:T(8,128)S(1)}, u32[]{:S(2)}) %copy-start.7) | copy-done | bytes 3145752
  76.1 0.0 copy-start.11
  76.1 1.2 copy-done.11
  77.3 0.0 copy-start.1
  77.3 0.0 collective-permute-done.1.caption_ref
  77.3 0.0 copy-start.12
  77.3 1.6 %copy-done.12 = bf16[1024,768]{1,0:T(8,128)(2,1)S(1)} copy-done((bf16[1024,768]{1,0:T(8,128)(2,1)S(1)}, bf16[1024,768]{1,0:T(8,128)(2,1)}, u32[]{:S(2)}) %copy-start.12) | copy-done | bytes 1572888
  78.9 10.1 %part_b.1 = (bf16[640,1024]{1,0:T(8,128)(2,1)S(1)}, bf16[640,1024]{1,0:T(8,128)(2,1)S(1)}, bf16[640,768]{1,0:T(8,128)(2,1)S(1)}, bf16[640,768]{1,0:T(8,128)(2,1)...) custom-call(f32[2]{0:T(128)S(1)} %pad_maximum_fusion.scal_ref, ...), custom_call_target="tpu_custom_call" | custom-call | flops 18119393280 | bytes 7864320 | tf_op jit(solution)/shard_map/part_b/pallas_call | solution.py:240
  89.0 2.1 %collective-permute-start.9 = (f32[384,768]{1,0:T(8,128)}, f32[384,768]{1,0:T(8,128)S(1)}, u32[]{:S(2)}, u32[]{:S(2)}) collective-permute-start(f32[384,768]{1,0:T(8,128)} %get-tuple-element.40), channel_id=1, source_target_pairs={{0,128},{32,160},{64,192},{96,224},{128,0},{160,32},{192,64},{224,... | collective-permute-start | bytes 3538952 | tf_op jit(solution)/shard_map/ppermute | solution.py:32
  91.1 1.4 collective-permute-start.8
  92.5 2.1 %collective-permute-start.7 = (f32[64,768]{1,0:T(8,128)S(1)}, f32[64,768]{1,0:T(8,128)S(1)}, u32[]{:S(2)}, u32[]{:S(2)}) collective-permute-start(f32[64,768]{1,0:T(8,128)S(1)} %get-tuple-element.38), channel_id=1, source_target_pairs={{0,128},{32,160},{64,192},{96,224},{128,0},{160,32},{192,64},{224,... | collective-permute-start | bytes 589832 | tf_op jit(solution)/shard_map/ppermute | solution.py:32
  94.6 0.0 copy-done.1
  94.6 0.0 copy-start.8
  94.6 1.9 %copy-done.8 = f32[1024,768]{1,0:T(8,128)S(1)} copy-done((f32[1024,768]{1,0:T(8,128)S(1)}, f32[1024,768]{1,0:T(8,128)}, u32[]{:S(2)}) %copy-start.8) | copy-done | bytes 3145752
  96.5 0.0 copy-start
  96.5 6.4 %image_grad.1 = f32[1024,768]{1,0:T(8,128)} custom-call(bf16[640,1024]{1,0:T(8,128)(2,1)S(1)} %get-tuple-element.32.g_hi_ref, bf16[640,1024]{1,0:T(8,128)(2,1)S(1)} %get-tuple-element.33.g_lo_ref, bf16[640,768]{1,0:T(8,128)(2,1)S(1)} %get-tuple-element.34.v_hi_ref, bf16[640,768]{1,0:T(8,128)(2,1)S(1)} %get-tuple-element.35.v_lo_ref, ...), custom_call_target="tpu_custom_call" | custom-call | flops 6039797760 | bytes 7864320 | tf_op jit(solution)/shard_map/image_grad/pallas_call | solution.py:255
  102.9 0.0 collective-permute-done.6.u_ref
  102.9 0.0 copy-done
  102.9 16.3 %cyc_images.1.base_ref = f32[1024,768]{1,0:T(8,128)S(1)} custom-call(f32[2]{0:T(128)S(1)} %pad_maximum_fusion.scal_ref, f32[1024,768]{1,0:T(8,128)} %collective-permute-done.6.u_ref, f32[1024,768]{1,0:T(8,128)S(1)} %copy-done, f32[1024,768]{1,0:T(8,128)} %get-tuple-element.37.dv_in_ref), custom_call_target="tpu_custom_call" | custom-call | flops 9663676416 | bytes 12582912 | tf_op jit(solution)/shard_map/cyc_images/pallas_call | solution.py:222
  119.2 0.0 collective-permute-done.10.part_ref
  119.2 1.4 %finish.4.rest_0_ = f32[1024,768]{1,0:T(8,128)} custom-call(f32[1024,768]{1,0:T(8,128)S(1)} %copy-done, f32[1024,768]{1,0:T(8,128)S(1)} %cyc_images.1.base_ref, f32[384,768]{1,0:T(8,128)S(1)} %collective-permute-done.10.part_ref), custom_call_target="tpu_custom_call" | custom-call | flops 2949120 | bytes 4718592 | tf_op jit(solution)/shard_map/finish/pallas_call | solution.py:272
  120.7 5.0 %collective-permute-done.9.part_ref = f32[384,768]{1,0:T(8,128)S(1)} collective-permute-done((f32[384,768]{1,0:T(8,128)}, f32[384,768]{1,0:T(8,128)S(1)}, u32[]{:S(2)}, u32[]{:S(2)}) %collective-permute-start.9) | collective-permute-done | bytes 1179680 | tf_op jit(solution)/shard_map/ppermute | solution.py:32
  125.7 1.4 finish.5.rest_0_
  127.1 11.2 %collective-permute-done.8.part_ref = f32[192,768]{1,0:T(8,128)S(1)} collective-permute-done((f32[192,768]{1,0:T(8,128)S(1)}, f32[192,768]{1,0:T(8,128)S(1)}, u32[]{:S(2)}, u32[]{:S(2)}) %collective-permute-start.8) | collective-permute-done | bytes 589856 | tf_op jit(solution)/shard_map/ppermute | solution.py:32
  138.3 1.1 finish.6.rest_0_
  139.4 2.0 %collective-permute-done.7.part_ref = f32[64,768]{1,0:T(8,128)S(1)} collective-permute-done((f32[64,768]{1,0:T(8,128)S(1)}, f32[64,768]{1,0:T(8,128)S(1)}, u32[]{:S(2)}, u32[]{:S(2)}) %collective-permute-start.7) | collective-permute-done | bytes 196640 | tf_op jit(solution)/shard_map/ppermute | solution.py:32
  141.4 0.9 finish.7
Async XLA Ops:
  0.6 17.6 %copy-start.6 = (s32[1024]{0:T(1024)S(1)}, s32[1024]{0:T(1024)}, u32[]{:S(2)}) copy-start(s32[1024]{0:T(1024)} %param.7) | copy-start | bytes 12292
  2.4 13.7 %collective-permute-start = (f32[128,768]{1,0:T(8,128)}, f32[128,768]{1,0:T(8,128)S(1)}, u32[]{:S(2)}, u32[]{:S(2)}) collective-permute-start(f32[128,768]{1,0:T(8,128)} %slice.9), channel_id=1, source_target_pairs={{0,128},{32,160},{64,192},{96,224},{128,0},{160,32},{192,64},{224,... | collective-permute-start | bytes 1179656 | tf_op jit(solution)/shard_map/ppermute | solution.py:32
  6.7 33.2 %collective-permute-start.5 = (f32[256,768]{1,0:T(8,128)}, f32[256,768]{1,0:T(8,128)S(1)}, u32[]{:S(2)}, u32[]{:S(2)}) collective-permute-start(f32[256,768]{1,0:T(8,128)} %slice.10), channel_id=1, source_target_pairs={{0,128},{32,160},{64,192},{96,224},{128,0},{160,32},{192,64},{224,... | collective-permute-start | bytes 2359304 | tf_op jit(solution)/shard_map/ppermute | solution.py:32
  8.1 51.8 %collective-permute-start.3 = (f32[256,768]{1,0:T(8,128)}, f32[256,768]{1,0:T(8,128)}, u32[]{:S(2)}, u32[]{:S(2)}) collective-permute-start(f32[256,768]{1,0:T(8,128)} %slice.10), channel_id=1, source_target_pairs={{31,0},{0,1},{1,2},{2,3},{3,4},{4,5},{5,6},{6,7},{7,8},{8,9},{9,10... | collective-permute-start | bytes 2359304 | tf_op jit(solution)/shard_map/ppermute | solution.py:27
  8.1 50.4 %collective-permute-start.2 = (f32[128,768]{1,0:T(8,128)}, f32[128,768]{1,0:T(8,128)S(1)}, u32[]{:S(2)}, u32[]{:S(2)}) collective-permute-start(f32[128,768]{1,0:T(8,128)} %slice.9), channel_id=1, source_target_pairs={{31,0},{0,1},{1,2},{2,3},{3,4},{4,5},{5,6},{6,7},{7,8},{8,9},{9,10... | collective-permute-start | bytes 1179656 | tf_op jit(solution)/shard_map/ppermute | solution.py:27
  12.8 47.1 %collective-permute-start.4 = (f32[640,768]{1,0:T(8,128)}, f32[640,768]{1,0:T(8,128)S(1)}, u32[]{:S(2)}, u32[]{:S(2)}) collective-permute-start(f32[640,768]{1,0:T(8,128)} %slice.11), channel_id=1, source_target_pairs={{31,0},{0,1},{1,2},{2,3},{3,4},{4,5},{5,6},{6,7},{7,8},{8,9},{9,10... | collective-permute-start | bytes 5898248 | tf_op jit(solution)/shard_map/ppermute | solution.py:27
  16.1 22.1 %copy-start.4 = (f32[128,768]{1,0:T(8,128)}, f32[128,768]{1,0:T(8,128)S(1)}, u32[]{:S(2)}) copy-start(f32[128,768]{1,0:T(8,128)S(1)} %collective-permute-done.after_ref.rest_0_) | copy-start | bytes 1179652
  16.1 61.2 %collective-permute-start.1 = (f32[640,768]{1,0:T(8,128)}, f32[640,768]{1,0:T(8,128)S(1)}, u32[]{:S(2)}, u32[]{:S(2)}) collective-permute-start(f32[640,768]{1,0:T(8,128)} %slice.11), channel_id=1, source_target_pairs={{0,128},{32,160},{64,192},{96,224},{128,0},{160,32},{192,64},{224,... | collective-permute-start | bytes 5898248 | tf_op jit(solution)/shard_map/ppermute | solution.py:32
  38.2 1.7 %copy-start.10 = (f32[1024,768]{1,0:T(8,128)}, f32[1024,768]{1,0:T(8,128)S(1)}, u32[]{:S(2)}) copy-start(f32[1024,768]{1,0:T(8,128)S(1)} %get-tuple-element.29.rest_2_) | copy-start | bytes 9437188
  39.9 0.9 copy-start.2
  40.8 1.1 copy-start.3
  41.9 1.0 copy-start.5
  54.9 1.7 %copy-start.9 = (f32[1024,768]{1,0:T(8,128)}, f32[1024,768]{1,0:T(8,128)S(1)}, u32[]{:S(2)}) copy-start(f32[1024,768]{1,0:T(8,128)S(1)} %get-tuple-element.31.rest_3_) | copy-start | bytes 9437188
  56.6 46.3 %collective-permute-start.6 = (f32[1024,768]{1,0:T(8,128)}, f32[1024,768]{1,0:T(8,128)}, u32[]{:S(2)}, u32[]{:S(2)}) collective-permute-start(f32[1024,768]{1,0:T(8,128)} %get-tuple-element.36), channel_id=1, source_target_pairs={{1,0},{2,1},{3,2},{4,3},{5,4},{6,5},{7,6},{8,7},{9,8},{10,9},{11,1... | collective-permute-start | bytes 9437192 | tf_op jit(solution)/shard_map/ppermute | solution.py:27
  58.5 60.7 %collective-permute-start.10 = (f32[384,768]{1,0:T(8,128)S(1)}, f32[384,768]{1,0:T(8,128)S(1)}, u32[]{:S(2)}, u32[]{:S(2)}) collective-permute-start(f32[384,768]{1,0:T(8,128)S(1)} %get-tuple-element.41), channel_id=1, source_target_pairs={{0,128},{32,160},{64,192},{96,224},{128,0},{160,32},{192,64},{224,... | collective-permute-start | bytes 3538952 | tf_op jit(solution)/shard_map/ppermute | solution.py:32
  74.5 1.7 %copy-start.7 = (f32[1024,768]{1,0:T(8,128)}, f32[1024,768]{1,0:T(8,128)S(1)}, u32[]{:S(2)}) copy-start(f32[1024,768]{1,0:T(8,128)S(1)} %cyc_captions.1.after_ref.du_ref) | copy-start | bytes 9437188
  76.1 1.2 copy-start.11
  77.3 17.3 %copy-start.1 = (f32[1024,768]{1,0:T(8,128)S(1)}, f32[1024,768]{1,0:T(8,128)}, u32[]{:S(2)}) copy-start(f32[1024,768]{1,0:T(8,128)} %image_ref.3) | copy-start | bytes 9437188
  77.3 1.6 %copy-start.12 = (bf16[1024,768]{1,0:T(8,128)(2,1)S(1)}, bf16[1024,768]{1,0:T(8,128)(2,1)}, u32[]{:S(2)}) copy-start(bf16[1024,768]{1,0:T(8,128)(2,1)} %copy-done.11) | copy-start | bytes 4718596
  89.0 36.7 %collective-permute-start.9 = (f32[384,768]{1,0:T(8,128)}, f32[384,768]{1,0:T(8,128)S(1)}, u32[]{:S(2)}, u32[]{:S(2)}) collective-permute-start(f32[384,768]{1,0:T(8,128)} %get-tuple-element.40), channel_id=1, source_target_pairs={{0,128},{32,160},{64,192},{96,224},{128,0},{160,32},{192,64},{224,... | collective-permute-start | bytes 3538952 | tf_op jit(solution)/shard_map/ppermute | solution.py:32
  91.1 47.2 %collective-permute-start.8 = (f32[192,768]{1,0:T(8,128)S(1)}, f32[192,768]{1,0:T(8,128)S(1)}, u32[]{:S(2)}, u32[]{:S(2)}) collective-permute-start(f32[192,768]{1,0:T(8,128)S(1)} %get-tuple-element.39), channel_id=1, source_target_pairs={{0,128},{32,160},{64,192},{96,224},{128,0},{160,32},{192,64},{224,... | collective-permute-start | bytes 1769480 | tf_op jit(solution)/shard_map/ppermute | solution.py:32
  92.5 48.9 %collective-permute-start.7 = (f32[64,768]{1,0:T(8,128)S(1)}, f32[64,768]{1,0:T(8,128)S(1)}, u32[]{:S(2)}, u32[]{:S(2)}) collective-permute-start(f32[64,768]{1,0:T(8,128)S(1)} %get-tuple-element.38), channel_id=1, source_target_pairs={{0,128},{32,160},{64,192},{96,224},{128,0},{160,32},{192,64},{224,... | collective-permute-start | bytes 589832 | tf_op jit(solution)/shard_map/ppermute | solution.py:32
  94.6 1.9 %copy-start.8 = (f32[1024,768]{1,0:T(8,128)S(1)}, f32[1024,768]{1,0:T(8,128)}, u32[]{:S(2)}) copy-start(f32[1024,768]{1,0:T(8,128)} %copy-done.7) | copy-start | bytes 9437188
  96.5 6.4 %copy-start = (f32[1024,768]{1,0:T(8,128)S(1)}, f32[1024,768]{1,0:T(8,128)}, u32[]{:S(2)}) copy-start(f32[1024,768]{1,0:T(8,128)} %caption_ref.11) | copy-start | bytes 9437188
where the time goes:
time: 143 us; the launch traced here: 142 us
  Pallas kernels  84 us (59%)
  waiting for transfers between devices  20.1 us (14%)
  local copies, waits for them, and re-layouts  19.6 us (14%)
  starting transfers between devices  16.4 us (11%)
  between operations  2.08 us (1%)
    pallas_call x2, Pallas kernels, score(): pl.pallas_call(functools.partial(score_kernel, len(chunks), len(extra), t...  26.5 us
    ppermute x7, waiting for transfers between devices, partner(): return lax.ppermute(block, axis, [(i, (i + n // 2) % n) for i in range(n)])  20.1 us
    pallas_call x1, Pallas kernels, own_block(): pl.pallas_call(own_kernel, grid=(rows // TILE,), in_specs=[SMEM, SMEM, wh...  19.9 us
    pallas_call x1, Pallas kernels, cycle_images(): pl.pallas_call(images_kernel, grid=(rows // TILE,), in_specs=[SMEM, whole...  16.3 us
    ppermute x7, starting transfers between devices, partner(): return lax.ppermute(block, axis, [(i, (i + n // 2) % n) for i in range(n)])  12.7 us
    unnamed x26, local copies, waits for them, and re-layouts  12.7 us
    pallas_call x1, Pallas kernels, returns(): pl.pallas_call(functools.partial(returns_kernel, tile), grid=(part // til...  10.1 us
    slice x3, local copies, waits for them, and re-layouts, body(): chunk, later = lax.optimization_barrier((later[a:b], later))  6.93 us
  transfers between devices with their start and end apart: 11, of which 4 were waited for; matrix products, arithmetic and copies ran while one was open for 4% of the time, Pallas kernels for 58%

commit v1 on v0

--- a/solution.py
+++ b/solution.py
@@ -9,7 +9,7 @@
 
 EPS = 1e-06
 TILE = 256
-VMEM = 42
+VMEM = 50
 CUTS = (128, 384)
 SCALE = dict(own=1.0, part_a=1.0, cyc_captions=1.0, part_b=3.0, rest=2.0)
 BACK = (768, 960)

time: 143 us -> 142 us (level)
  local copies, waits for them, and re-layouts: 19.6 us -> 8.92 us
  Pallas kernels: 84 us -> 94 us
    unnamed x26 -> x12, local copies, waits for them, and re-layouts: 12.7 us -> 3.76 us
    pallas_call x2, Pallas kernels: 26.5 us -> 31.3 us  [score(): pl.pallas_call(functools.partial(score_kernel, len(chunks), len(extra), t...]
    slice x3, local copies, waits for them, and re-layouts: 6.93 us -> 5.16 us  [body(): chunk, later = lax.optimization_barrier((later[a:b], later))]
    pallas_call x1, Pallas kernels: 6.38 us -> 8.12 us  [image_gradient(): pl.pallas_call(rest_kernel, grid=(rows // TILE,), in_specs=[pl.BlockSpec(...]
    pallas_call x1, Pallas kernels: 10.1 us -> 11.7 us  [returns(): pl.pallas_call(functools.partial(returns_kernel, tile), grid=(part // til...]
  transfers between devices with their start and end apart: 11 -> 11, of which waited for: 4 -> 5; matrix products, arithmetic and copies ran while one was open for 4% -> 3% of each run, Pallas kernels for 58% -> 66%
where the time goes in v1:
time: 142 us; the launch traced here: 141 us
  Pallas kernels  94 us (66%)
  waiting for transfers between devices  20.6 us (15%)
  starting transfers between devices  15.8 us (11%)
  local copies, waits for them, and re-layouts  8.92 us (6%)
  between operations  2.03 us (1%)
    pallas_call x2, Pallas kernels, score(): pl.pallas_call(functools.partial(score_kernel, len(chunks), len(extra), t...  31.3 us
    pallas_call x1, Pallas kernels, own_block(): pl.pallas_call(own_kernel, grid=(rows // TILE,), in_specs=[SMEM, SMEM, wh...  21.4 us
    ppermute x7, waiting for transfers between devices, partner(): return lax.ppermute(block, axis, [(i, (i + n // 2) % n) for i in range(n)])  20.6 us
    pallas_call x1, Pallas kernels, cycle_images(): pl.pallas_call(images_kernel, grid=(rows // TILE,), in_specs=[SMEM, whole...  16.7 us
    ppermute x7, starting transfers between devices, partner(): return lax.ppermute(block, axis, [(i, (i + n // 2) % n) for i in range(n)])  12.9 us
    pallas_call x1, Pallas kernels, returns(): pl.pallas_call(functools.partial(returns_kernel, tile), grid=(part // til...  11.7 us
    pallas_call x1, Pallas kernels, image_gradient(): pl.pallas_call(rest_kernel, grid=(rows // TILE,), in_specs=[pl.BlockSpec(...  8.12 us
    slice x3, local copies, waits for them, and re-layouts, body(): chunk, later = lax.optimization_barrier((later[a:b], later))  5.16 us
  transfers between devices with their start and end apart: 11, of which 5 were waited for; matrix products, arithmetic and copies ran while one was open for 3% of the time, Pallas kernels for 66%

profile of v1, /device:TPU:130, one launch (start us, length us, event | category | flops | bytes accessed | tf_op | source)
XLA Modules:
  0.0 141.4 jit_solution(5344156113690978190)
XLA Ops:
  0.6 0.0 copy-start.1
  0.6 1.0 slice.9
  1.7 2.2 %collective-permute-start = (f32[128,768]{1,0:T(8,128)S(1)}, f32[128,768]{1,0:T(8,128)S(1)}, u32[]{:S(2)}, u32[]{:S(2)}) collective-permute-start(f32[128,768]{1,0:T(8,128)S(1)} %slice.9), channel_id=1, source_target_pairs={{0,128},{32,160},{64,192},{96,224},{128,0},{160,32},{192,64},{224,... | collective-permute-start | bytes 1179656 | tf_op jit(solution)/shard_map/ppermute | solution.py:32
  3.9 1.2 slice.10
  5.1 1.5 %collective-permute-start.5 = (f32[256,768]{1,0:T(8,128)S(1)}, f32[256,768]{1,0:T(8,128)S(1)}, u32[]{:S(2)}, u32[]{:S(2)}) collective-permute-start(f32[256,768]{1,0:T(8,128)S(1)} %slice.10), channel_id=1, source_target_pairs={{0,128},{32,160},{64,192},{96,224},{128,0},{160,32},{192,64},{224,... | collective-permute-start | bytes 2359304 | tf_op jit(solution)/shard_map/ppermute | solution.py:32
  6.6 0.0 collective-permute-start.3
  6.6 1.7 %collective-permute-start.2 = (f32[128,768]{1,0:T(8,128)S(1)}, f32[128,768]{1,0:T(8,128)S(1)}, u32[]{:S(2)}, u32[]{:S(2)}) collective-permute-start(f32[128,768]{1,0:T(8,128)S(1)} %slice.9), channel_id=1, source_target_pairs={{31,0},{0,1},{1,2},{2,3},{3,4},{4,5},{5,6},{6,7},{7,8},{8,9},{9,10... | collective-permute-start | bytes 1179656 | tf_op jit(solution)/shard_map/ppermute | solution.py:27
  8.3 3.0 %slice.11 = f32[640,768]{1,0:T(8,128)} slice(f32[1024,768]{1,0:T(8,128)} %caption_ref.11), slice={[384:1024], [0:768]} | slice | bytes 3932160 | tf_op jit(solution)/shard_map/slice | solution.py:289
  11.2 0.0 collective-permute-start.4
  12.6 0.1 pad_maximum_fusion.scal_ref
  12.7 2.6 %collective-permute-done.after_ref.rest_0_ = f32[128,768]{1,0:T(8,128)S(1)} collective-permute-done((f32[128,768]{1,0:T(8,128)S(1)}, f32[128,768]{1,0:T(8,128)S(1)}, u32[]{:S(2)}, u32[]{:S(2)}) %collective-permute-start) | collective-permute-done | bytes 393248 | tf_op jit(solution)/shard_map/ppermute | solution.py:32
  15.3 2.1 %collective-permute-start.1 = (f32[640,768]{1,0:T(8,128)}, f32[640,768]{1,0:T(8,128)S(1)}, u32[]{:S(2)}, u32[]{:S(2)}) collective-permute-start(f32[640,768]{1,0:T(8,128)} %slice.11), channel_id=1, source_target_pairs={{0,128},{32,160},{64,192},{96,224},{128,0},{160,32},{192,64},{224,... | collective-permute-start | bytes 5898248 | tf_op jit(solution)/shard_map/ppermute | solution.py:32
  17.4 0.0 copy-done.1
  17.4 21.4 %own.1 = (f32[1024,768]{1,0:T(8,128)}, bf16[1024,768]{1,0:T(8,128)(2,1)S(1)}, bf16[1024,768]{1,0:T(8,128)(2,1)S(1)}, f32[1024,768]{1,0:T(8,128)}, f32[1024,768]{1,0:T(8,128)}) custom-call(s32[1]{0:T(128)} %bitcast.first_ref, f32[2]{0:T(128)S(1)} %pad_maximum_fusion.scal_ref, s32[1,1024]{1,0:T(1,128)S(1)} %bitcast.2, f32[1024,768]{1,0:T(8,128)} %image_ref.3, ...), custom_call_target="tpu_custom_call" | custom-call | flops 14495514624 | bytes 12582912 | tf_op jit(solution)/shard_map/own/pallas_call | solution.py:188
  38.8 0.0 copy-start.4
  38.8 1.2 copy-done.4
  39.9 0.0 copy-start.3
  39.9 0.0 collective-permute-done.5.rest_1_
  39.9 14.6 %part_a.1 = (f32[1024,768]{1,0:T(8,128)}, f32[1024,768]{1,0:T(8,128)}, f32[384,768]{1,0:T(8,128)S(1)}) custom-call(f32[2]{0:T(128)S(1)} %pad_maximum_fusion.scal_ref, bf16[1024,768]{1,0:T(8,128)(2,1)S(1)} %get-tuple-element.23.hi_ref, bf16[1024,768]{1,0:T(8,128)(2,1)} %copy-done.4, ...), custom_call_target="tpu_custom_call", output_to_operand_aliasing={{1}: (6, {})} | custom-call | flops 5435817984 | bytes 4718592 | tf_op jit(solution)/shard_map/part_a/pallas_call | solution.py:206
  54.5 1.1 collective-permute-start.6
  55.6 0.0 collective-permute-done.2.rest_0_
  55.6 1.4 collective-permute-start.10
  57.1 0.0 collective-permute-done.3.rest_1_
  57.1 0.0 collective-permute-done.4.rest_2_
  57.1 0.0 copy-done.3
  57.1 16.7 %cyc_captions.1.after_ref.du_ref = f32[1024,768]{1,0:T(8,128)} custom-call(f32[2]{0:T(128)S(1)} %pad_maximum_fusion.scal_ref, bf16[1024,768]{1,0:T(8,128)(2,1)S(1)} %get-tuple-element.23.hi_ref, bf16[1024,768]{1,0:T(8,128)(2,1)} %copy-done.4, f32[128,768]{1,0:T(8,128)S(1)} %collective-permute-done.2.rest_0_, f32[256,768]{1,0:T(8,128)S(1)} %collective-permute-done.3.rest_1_, ...), custom_call_target="tpu_custom_call" | custom-call | flops 9663676416 | bytes 12582912 | tf_op jit(solution)/shard_map/cyc_captions/pallas_call | solution.py:206
  73.7 0.5 collective-permute-done.1.caption_ref
  74.2 0.0 copy-start.5
  74.3 1.3 copy-done.5
  75.5 11.7 %part_b.1 = (bf16[640,1024]{1,0:T(8,128)(2,1)}, bf16[640,1024]{1,0:T(8,128)(2,1)}, bf16[640,768]{1,0:T(8,128)(2,1)S(1)}, bf16[640,768]{1,0:T(8,128)(2,1)S(1)}, f...) custom-call(f32[2]{0:T(128)S(1)} %pad_maximum_fusion.scal_ref, bf16[1024,768]{1,0:T(8,128)(2,1)} %copy-done.3, ...), custom_call_target="tpu_custom_call" | custom-call | flops 18119393280 | bytes 7864320 | tf_op jit(solution)/shard_map/part_b/pallas_call | solution.py:240
  87.2 2.1 %collective-permute-start.9 = (f32[384,768]{1,0:T(8,128)S(1)}, f32[384,768]{1,0:T(8,128)S(1)}, u32[]{:S(2)}, u32[]{:S(2)}) collective-permute-start(f32[384,768]{1,0:T(8,128)S(1)} %get-tuple-element.40), channel_id=1, source_target_pairs={{0,128},{32,160},{64,192},{96,224},{128,0},{160,32},{192,64},{224,... | collective-permute-start | bytes 3538952 | tf_op jit(solution)/shard_map/ppermute | solution.py:32
  89.4 1.4 collective-permute-start.8
  90.8 2.1 %collective-permute-start.7 = (f32[64,768]{1,0:T(8,128)S(1)}, f32[64,768]{1,0:T(8,128)S(1)}, u32[]{:S(2)}, u32[]{:S(2)}) collective-permute-start(f32[64,768]{1,0:T(8,128)S(1)} %get-tuple-element.38), channel_id=1, source_target_pairs={{0,128},{32,160},{64,192},{96,224},{128,0},{160,32},{192,64},{224,... | collective-permute-start | bytes 589832 | tf_op jit(solution)/shard_map/ppermute | solution.py:32
  92.9 0.0 copy-start.2
  92.9 1.3 copy-done.2
  94.2 8.1 %image_grad.1 = f32[1024,768]{1,0:T(8,128)} custom-call(bf16[640,1024]{1,0:T(8,128)(2,1)S(1)} %copy-done.2, bf16[640,1024]{1,0:T(8,128)(2,1)} %get-tuple-element.33.g_lo_ref, bf16[640,768]{1,0:T(8,128)(2,1)S(1)} %get-tuple-element.34.v_hi_ref, bf16[640,768]{1,0:T(8,128)(2,1)S(1)} %get-tuple-element.35.v_lo_ref, f32[1024,768]{1,0:T(8,128)} %cyc_captions.1.after_ref.du_ref, ...), custom_call_target="tpu_custom_call" | custom-call | flops 6039797760 | bytes 7864320 | tf_op jit(solution)/shard_map/image_grad/pallas_call | solution.py:255
  102.3 0.0 collective-permute-done.6.u_ref
  102.3 0.0 copy-start
  102.3 16.7 %cyc_images.1.base_ref = f32[1024,768]{1,0:T(8,128)S(1)} custom-call(f32[2]{0:T(128)S(1)} %pad_maximum_fusion.scal_ref, f32[1024,768]{1,0:T(8,128)} %collective-permute-done.6.u_ref, f32[1024,768]{1,0:T(8,128)} %caption_ref.11, f32[1024,768]{1,0:T(8,128)} %get-tuple-element.37.dv_in_ref), custom_call_target="tpu_custom_call" | custom-call | flops 9663676416 | bytes 12582912 | tf_op jit(solution)/shard_map/cyc_images/pallas_call | solution.py:222
  119.1 0.0 collective-permute-done.10.part_ref
  119.1 0.0 copy-done
  119.1 1.4 %finish.4.rest_0_ = f32[1024,768]{1,0:T(8,128)} custom-call(f32[1024,768]{1,0:T(8,128)S(1)} %copy-done, f32[1024,768]{1,0:T(8,128)S(1)} %cyc_images.1.base_ref, f32[384,768]{1,0:T(8,128)S(1)} %collective-permute-done.10.part_ref), custom_call_target="tpu_custom_call" | custom-call | flops 2949120 | bytes 4718592 | tf_op jit(solution)/shard_map/finish/pallas_call | solution.py:272
  120.5 4.3 %collective-permute-done.9.part_ref = f32[384,768]{1,0:T(8,128)S(1)} collective-permute-done((f32[384,768]{1,0:T(8,128)S(1)}, f32[384,768]{1,0:T(8,128)S(1)}, u32[]{:S(2)}, u32[]{:S(2)}) %collective-permute-start.9) | collective-permute-done | bytes 1179680 | tf_op jit(solution)/shard_map/ppermute | solution.py:32
  124.8 1.4 %finish.5.rest_0_ = f32[1024,768]{1,0:T(8,128)} custom-call(f32[1024,768]{1,0:T(8,128)S(1)} %copy-done, f32[1024,768]{1,0:T(8,128)S(1)} %cyc_images.1.base_ref, f32[384,768]{1,0:T(8,128)S(1)} %collective-permute-done.9.part_ref, f32[1024,768]{1,0:T(8,128)} %finish.4.rest_0_), custom_call_target="tpu_custom_call", output_to_operand_aliasing={{}: (3, {})} | custom-call | flops 2949120 | bytes 4718592 | tf_op jit(solution)/shard_map/finish/pallas_call | solution.py:272
  126.2 11.2 %collective-permute-done.8.part_ref = f32[192,768]{1,0:T(8,128)S(1)} collective-permute-done((f32[192,768]{1,0:T(8,128)S(1)}, f32[192,768]{1,0:T(8,128)S(1)}, u32[]{:S(2)}, u32[]{:S(2)}) %collective-permute-start.8) | collective-permute-done | bytes 589856 | tf_op jit(solution)/shard_map/ppermute | solution.py:32
  137.4 1.1 finish.6.rest_0_
  138.6 2.0 %collective-permute-done.7.part_ref = f32[64,768]{1,0:T(8,128)S(1)} collective-permute-done((f32[64,768]{1,0:T(8,128)S(1)}, f32[64,768]{1,0:T(8,128)S(1)}, u32[]{:S(2)}, u32[]{:S(2)}) %collective-permute-start.7) | collective-permute-done | bytes 196640 | tf_op jit(solution)/shard_map/ppermute | solution.py:32
  140.5 0.9 finish.7
Async XLA Ops:
  0.6 16.8 %copy-start.1 = (s32[1024]{0:T(1024)S(1)}, s32[1024]{0:T(1024)}, u32[]{:S(2)}) copy-start(s32[1024]{0:T(1024)} %param.7) | copy-start | bytes 12292
  1.7 13.6 %collective-permute-start = (f32[128,768]{1,0:T(8,128)S(1)}, f32[128,768]{1,0:T(8,128)S(1)}, u32[]{:S(2)}, u32[]{:S(2)}) collective-permute-start(f32[128,768]{1,0:T(8,128)S(1)} %slice.9), channel_id=1, source_target_pairs={{0,128},{32,160},{64,192},{96,224},{128,0},{160,32},{192,64},{224,... | collective-permute-start | bytes 1179656 | tf_op jit(solution)/shard_map/ppermute | solution.py:32
  5.1 34.8 %collective-permute-start.5 = (f32[256,768]{1,0:T(8,128)S(1)}, f32[256,768]{1,0:T(8,128)S(1)}, u32[]{:S(2)}, u32[]{:S(2)}) collective-permute-start(f32[256,768]{1,0:T(8,128)S(1)} %slice.10), channel_id=1, source_target_pairs={{0,128},{32,160},{64,192},{96,224},{128,0},{160,32},{192,64},{224,... | collective-permute-start | bytes 2359304 | tf_op jit(solution)/shard_map/ppermute | solution.py:32
  6.6 50.5 %collective-permute-start.3 = (f32[256,768]{1,0:T(8,128)S(1)}, f32[256,768]{1,0:T(8,128)S(1)}, u32[]{:S(2)}, u32[]{:S(2)}) collective-permute-start(f32[256,768]{1,0:T(8,128)S(1)} %slice.10), channel_id=1, source_target_pairs={{31,0},{0,1},{1,2},{2,3},{3,4},{4,5},{5,6},{6,7},{7,8},{8,9},{9,10... | collective-permute-start | bytes 2359304 | tf_op jit(solution)/shard_map/ppermute | solution.py:27
  6.6 49.1 %collective-permute-start.2 = (f32[128,768]{1,0:T(8,128)S(1)}, f32[128,768]{1,0:T(8,128)S(1)}, u32[]{:S(2)}, u32[]{:S(2)}) collective-permute-start(f32[128,768]{1,0:T(8,128)S(1)} %slice.9), channel_id=1, source_target_pairs={{31,0},{0,1},{1,2},{2,3},{3,4},{4,5},{5,6},{6,7},{7,8},{8,9},{9,10... | collective-permute-start | bytes 1179656 | tf_op jit(solution)/shard_map/ppermute | solution.py:27
  11.2 45.9 %collective-permute-start.4 = (f32[640,768]{1,0:T(8,128)}, f32[640,768]{1,0:T(8,128)}, u32[]{:S(2)}, u32[]{:S(2)}) collective-permute-start(f32[640,768]{1,0:T(8,128)} %slice.11), channel_id=1, source_target_pairs={{31,0},{0,1},{1,2},{2,3},{3,4},{4,5},{5,6},{6,7},{7,8},{8,9},{9,10... | collective-permute-start | bytes 5898248 | tf_op jit(solution)/shard_map/ppermute | solution.py:27
  15.3 59.0 %collective-permute-start.1 = (f32[640,768]{1,0:T(8,128)}, f32[640,768]{1,0:T(8,128)S(1)}, u32[]{:S(2)}, u32[]{:S(2)}) collective-permute-start(f32[640,768]{1,0:T(8,128)} %slice.11), channel_id=1, source_target_pairs={{0,128},{32,160},{64,192},{96,224},{128,0},{160,32},{192,64},{224,... | collective-permute-start | bytes 5898248 | tf_op jit(solution)/shard_map/ppermute | solution.py:32
  38.8 1.2 copy-start.4
  39.9 17.1 %copy-start.3 = (bf16[1024,768]{1,0:T(8,128)(2,1)}, bf16[1024,768]{1,0:T(8,128)(2,1)S(1)}, u32[]{:S(2)}) copy-start(bf16[1024,768]{1,0:T(8,128)(2,1)S(1)} %get-tuple-element.23.hi_ref) | copy-start | bytes 4718596
  54.5 47.8 %collective-permute-start.6 = (f32[1024,768]{1,0:T(8,128)}, f32[1024,768]{1,0:T(8,128)}, u32[]{:S(2)}, u32[]{:S(2)}) collective-permute-start(f32[1024,768]{1,0:T(8,128)} %get-tuple-element.36), channel_id=1, source_target_pairs={{1,0},{2,1},{3,2},{4,3},{5,4},{6,5},{7,6},{8,7},{9,8},{10,9},{11,1... | collective-permute-start | bytes 9437192 | tf_op jit(solution)/shard_map/ppermute | solution.py:27
  55.6 63.4 %collective-permute-start.10 = (f32[384,768]{1,0:T(8,128)S(1)}, f32[384,768]{1,0:T(8,128)S(1)}, u32[]{:S(2)}, u32[]{:S(2)}) collective-permute-start(f32[384,768]{1,0:T(8,128)S(1)} %get-tuple-element.41), channel_id=1, source_target_pairs={{0,128},{32,160},{64,192},{96,224},{128,0},{160,32},{192,64},{224,... | collective-permute-start | bytes 3538952 | tf_op jit(solution)/shard_map/ppermute | solution.py:32
  74.2 1.3 copy-start.5
  87.2 37.6 %collective-permute-start.9 = (f32[384,768]{1,0:T(8,128)S(1)}, f32[384,768]{1,0:T(8,128)S(1)}, u32[]{:S(2)}, u32[]{:S(2)}) collective-permute-start(f32[384,768]{1,0:T(8,128)S(1)} %get-tuple-element.40), channel_id=1, source_target_pairs={{0,128},{32,160},{64,192},{96,224},{128,0},{160,32},{192,64},{224,... | collective-permute-start | bytes 3538952 | tf_op jit(solution)/shard_map/ppermute | solution.py:32
  89.4 48.1 %collective-permute-start.8 = (f32[192,768]{1,0:T(8,128)S(1)}, f32[192,768]{1,0:T(8,128)S(1)}, u32[]{:S(2)}, u32[]{:S(2)}) collective-permute-start(f32[192,768]{1,0:T(8,128)S(1)} %get-tuple-element.39), channel_id=1, source_target_pairs={{0,128},{32,160},{64,192},{96,224},{128,0},{160,32},{192,64},{224,... | collective-permute-start | bytes 1769480 | tf_op jit(solution)/shard_map/ppermute | solution.py:32
  90.8 49.8 %collective-permute-start.7 = (f32[64,768]{1,0:T(8,128)S(1)}, f32[64,768]{1,0:T(8,128)S(1)}, u32[]{:S(2)}, u32[]{:S(2)}) collective-permute-start(f32[64,768]{1,0:T(8,128)S(1)} %get-tuple-element.38), channel_id=1, source_target_pairs={{0,128},{32,160},{64,192},{96,224},{128,0},{160,32},{192,64},{224,... | collective-permute-start | bytes 589832 | tf_op jit(solution)/shard_map/ppermute | solution.py:32
  92.9 1.3 copy-start.2
  102.3 16.7 %copy-start = (f32[1024,768]{1,0:T(8,128)S(1)}, f32[1024,768]{1,0:T(8,128)}, u32[]{:S(2)}) copy-start(f32[1024,768]{1,0:T(8,128)} %caption_ref.11) | copy-start | bytes 9437188

commit v2 on v1

--- a/solution.py
+++ b/solution.py
@@ -145,7 +145,9 @@
     grad_ref[...] = projected(image_ref[...], du)
 
 
-def images_kernel(scal_ref, u_ref, caption_ref, dv_in_ref, dv_ref, hi_ref, lo_ref):
+def images_kernel(scal_ref, u_ref, caption_ref, dv_in_ref, after_ref, dv_ref, hi_ref, lo_ref):
+    del after_ref
+
     @pl.when(pl.program_id(0) == 0)
     def _():
         hi_ref[...], lo_ref[...] = split(u_ref[...])
@@ -157,6 +159,23 @@
 
 def finish_kernel(caption_ref, base_ref, part_ref, *rest):
     rest[-1][...] = projected(caption_ref[...], base_ref[...] + part_ref[...])
+
+
+def ready_kernel(caption_ref, base_ref, one_ref, r_ref, done_ref):
+    raw = caption_ref[...]
+    r = 1.0 / norm_of(raw)
+    one_ref[...] = raw * r
+    r_ref[...] = jnp.broadcast_to(r, r_ref.shape)
+    done_ref[...] = projected(raw, base_ref[...])
+
+
+def end_kernel(at, one_ref, r_ref, done_ref, part_ref, grad_in_ref, grad_ref, out_ref, sem):
+    del grad_in_ref
+    one, part = one_ref[...], part_ref[...]
+    out_ref[...] = done_ref[...] + (part - one * jnp.sum(one * part, axis=-1, keepdims=True)) * r_ref[:, :1]
+    copy = pltpu.make_async_copy(out_ref, grad_ref.at[pl.ds(at, out_ref.shape[0]), :], sem)
+    copy.start()
+    copy.wait()
 
 
 def whole(shape):
@@ -217,19 +236,19 @@
     )(scal, *u, *chunks, du, *extra)
 
 
-def cycle_images(scal, u, caption, dv):
+def cycle_images(scal, u, caption, dv, after):
     rows, d = dv.shape
     return pl.pallas_call(
         images_kernel,
         grid=(rows // TILE,),
-        in_specs=[SMEM, whole((rows, d)), blocks(TILE, d), blocks(TILE, d)],
+        in_specs=[SMEM, whole((rows, d)), blocks(TILE, d), blocks(TILE, d), pl.BlockSpec(memory_space=pl.ANY)],
         out_specs=blocks(TILE, d),
         out_shape=shape(rows, d),
         scratch_shapes=halves(rows, d),
         compiler_params=PARAMS,
         cost_estimate=cost(2, rows, rows, d),
         name="cyc_images",
-    )(scal, u, caption, dv)
+    )(scal, u, caption, dv, after)
 
 
 def returns(scal, u, captions, pieces, after):
@@ -280,6 +299,33 @@
         cost_estimate=pl.CostEstimate(flops=10 * part.size, bytes_accessed=16 * part.size, transcendentals=0),
         name="finish",
     )(caption, base, part, *([grad] if more else []))
+
+
+def end(caption, base, part, at, grad):
+    rows, d = caption.shape
+    n = part.shape[0]
+    one, r, done = pl.pallas_call(
+        ready_kernel,
+        grid=(1,),
+        in_specs=[blocks(n, d, at // n)] * 2,
+        out_specs=[blocks(n, d), blocks(n, 128), blocks(n, d)],
+        out_shape=[shape(n, d), shape(n, 128), shape(n, d)],
+        compiler_params=SMALL,
+        cost_estimate=pl.CostEstimate(flops=10 * part.size, bytes_accessed=16 * part.size, transcendentals=0),
+        name="ready",
+    )(caption, base)
+    local, anywhere = pl.BlockSpec(memory_space=pltpu.VMEM), pl.BlockSpec(memory_space=pl.ANY)
+    return pl.pallas_call(
+        functools.partial(end_kernel, at),
+        in_specs=[local] * 4 + [anywhere],
+        out_specs=anywhere,
+        out_shape=shape(rows, d),
+        scratch_shapes=[pltpu.VMEM((n, d), F32), pltpu.SemaphoreType.DMA],
+        input_output_aliases={4: 0},
+        compiler_params=SMALL,
+        cost_estimate=pl.CostEstimate(flops=10 * part.size, bytes_accessed=16 * part.size, transcendentals=0),
+        name="end",
+    )(one, r, done, part, grad)
 
 
 def body(image_embed, caption_embed, pair_ids, log_scale, logit_bias):
@@ -302,11 +348,12 @@
     pieces = [b - a for a, b in zip(edges, edges[1:])]
     g_hi, g_lo, v_hi, v_lo, *dv_part1 = returns(scal, u, parts[-1], pieces, du)
     backs = [partner(piece, "grp") for piece in dv_part1]
-    base = cycle_images(scal, next_u, caption_embed, dv)
     image_grad = image_gradient((g_hi, g_lo), (v_hi, v_lo), du, image_embed)
+    base = cycle_images(scal, next_u, caption_embed, dv, image_grad)
     grad = finish(caption_embed, base, back0, 0)
-    for at, back in zip(edges, backs):
+    for at, back in zip(edges[:-2], backs):
         grad = finish(caption_embed, base, back, at, grad)
+    grad = end(caption_embed, base, backs[-1], edges[-2], grad)
     return (image_grad, grad)
 
 

time: 142 us -> 142 us (level)
    pallas_call x4 -> x3, Pallas kernels: 4.86 us -> 3.97 us  [finish(): pl.pallas_call(finish_kernel, grid=(n // tile,), in_specs=[blocks(tile, d...]
where the time goes in v2:
time: 142 us
  Pallas kernels  94.2 us (66%)
  waiting for transfers between devices  20.4 us (14%)
  starting transfers between devices  15.8 us (11%)
  local copies, waits for them, and re-layouts  8.91 us (6%)
  between operations  2.24 us (2%)
    pallas_call x2, Pallas kernels, score(): pl.pallas_call(functools.partial(score_kernel, len(chunks), len(extra), t...  31.3 us
    pallas_call x1, Pallas kernels, own_block(): pl.pallas_call(own_kernel, grid=(rows // TILE,), in_specs=[SMEM, SMEM, wh...  21.4 us
    ppermute x7, waiting for transfers between devices, partner(): return lax.ppermute(block, axis, [(i, (i + n // 2) % n) for i in range(n)])  20.4 us
    pallas_call x1, Pallas kernels, cycle_images(): pl.pallas_call(images_kernel, grid=(rows // TILE,), in_specs=[SMEM, whole...  16.7 us
    ppermute x7, starting transfers between devices, partner(): return lax.ppermute(block, axis, [(i, (i + n // 2) % n) for i in range(n)])  12.9 us
    pallas_call x1, Pallas kernels, returns(): pl.pallas_call(functools.partial(returns_kernel, tile), grid=(part // til...  11.7 us
    pallas_call x1, Pallas kernels, image_gradient(): pl.pallas_call(rest_kernel, grid=(rows // TILE,), in_specs=[pl.BlockSpec(...  8.12 us
    slice x3, local copies, waits for them, and re-layouts, body(): chunk, later = lax.optimization_barrier((later[a:b], later))  5.16 us
  transfers between devices with their start and end apart: 11, of which 5 were waited for; matrix products, arithmetic and copies ran while one was open for 3% of the time, Pallas kernels for 66%

profile of v2, /device:TPU:130, one launch (start us, length us, event | category | flops | bytes accessed | tf_op | source)
XLA Modules:
  0.0 141.5 jit_solution(469120015311530915)
XLA Ops:
  0.6 0.0 copy-start.1
  0.6 1.0 slice.9
  1.7 2.2 %collective-permute-start = (f32[128,768]{1,0:T(8,128)S(1)}, f32[128,768]{1,0:T(8,128)S(1)}, u32[]{:S(2)}, u32[]{:S(2)}) collective-permute-start(f32[128,768]{1,0:T(8,128)S(1)} %slice.9), channel_id=1, source_target_pairs={{0,128},{32,160},{64,192},{96,224},{128,0},{160,32},{192,64},{224,... | collective-permute-start | bytes 1179656 | tf_op jit(solution)/shard_map/ppermute | solution.py:32
  3.9 1.2 slice.10
  5.1 1.5 %collective-permute-start.5 = (f32[256,768]{1,0:T(8,128)S(1)}, f32[256,768]{1,0:T(8,128)S(1)}, u32[]{:S(2)}, u32[]{:S(2)}) collective-permute-start(f32[256,768]{1,0:T(8,128)S(1)} %slice.10), channel_id=1, source_target_pairs={{0,128},{32,160},{64,192},{96,224},{128,0},{160,32},{192,64},{224,... | collective-permute-start | bytes 2359304 | tf_op jit(solution)/shard_map/ppermute | solution.py:32
  6.6 0.0 collective-permute-start.3
  6.6 1.7 %collective-permute-start.2 = (f32[128,768]{1,0:T(8,128)S(1)}, f32[128,768]{1,0:T(8,128)S(1)}, u32[]{:S(2)}, u32[]{:S(2)}) collective-permute-start(f32[128,768]{1,0:T(8,128)S(1)} %slice.9), channel_id=1, source_target_pairs={{31,0},{0,1},{1,2},{2,3},{3,4},{4,5},{5,6},{6,7},{7,8},{8,9},{9,10... | collective-permute-start | bytes 1179656 | tf_op jit(solution)/shard_map/ppermute | solution.py:27
  8.3 2.9 %slice.11 = f32[640,768]{1,0:T(8,128)} slice(f32[1024,768]{1,0:T(8,128)} %caption_ref.11), slice={[384:1024], [0:768]} | slice | bytes 3932160 | tf_op jit(solution)/shard_map/slice | solution.py:335
  11.2 0.0 collective-permute-start.4
  12.6 0.1 pad_maximum_fusion.scal_ref
  12.7 2.6 %collective-permute-done.after_ref.rest_0_ = f32[128,768]{1,0:T(8,128)S(1)} collective-permute-done((f32[128,768]{1,0:T(8,128)S(1)}, f32[128,768]{1,0:T(8,128)S(1)}, u32[]{:S(2)}, u32[]{:S(2)}) %collective-permute-start) | collective-permute-done | bytes 393248 | tf_op jit(solution)/shard_map/ppermute | solution.py:32
  15.3 2.1 %collective-permute-start.1 = (f32[640,768]{1,0:T(8,128)}, f32[640,768]{1,0:T(8,128)S(1)}, u32[]{:S(2)}, u32[]{:S(2)}) collective-permute-start(f32[640,768]{1,0:T(8,128)} %slice.11), channel_id=1, source_target_pairs={{0,128},{32,160},{64,192},{96,224},{128,0},{160,32},{192,64},{224,... | collective-permute-start | bytes 5898248 | tf_op jit(solution)/shard_map/ppermute | solution.py:32
  17.4 0.0 copy-done.1
  17.4 21.4 %own.1 = (f32[1024,768]{1,0:T(8,128)}, bf16[1024,768]{1,0:T(8,128)(2,1)S(1)}, bf16[1024,768]{1,0:T(8,128)(2,1)S(1)}, f32[1024,768]{1,0:T(8,128)}, f32[1024,768]{1,0:T(8,128)}) custom-call(s32[1]{0:T(128)} %bitcast.first_ref, f32[2]{0:T(128)S(1)} %pad_maximum_fusion.scal_ref, s32[1,1024]{1,0:T(1,128)S(1)} %bitcast.2, f32[1024,768]{1,0:T(8,128)} %image_ref.3, ...), custom_call_target="tpu_custom_call" | custom-call | flops 14495514624 | bytes 12582912 | tf_op jit(solution)/shard_map/own/pallas_call | solution.py:207
  38.8 0.0 copy-start.4
  38.8 1.2 copy-done.4
  39.9 0.0 copy-start.3
  39.9 0.0 collective-permute-done.5.rest_1_
  39.9 14.6 %part_a.1 = (f32[1024,768]{1,0:T(8,128)}, f32[1024,768]{1,0:T(8,128)}, f32[384,768]{1,0:T(8,128)S(1)}) custom-call(f32[2]{0:T(128)S(1)} %pad_maximum_fusion.scal_ref, bf16[1024,768]{1,0:T(8,128)(2,1)S(1)} %get-tuple-element.26.hi_ref, bf16[1024,768]{1,0:T(8,128)(2,1)} %copy-done.4, ...), custom_call_target="tpu_custom_call", output_to_operand_aliasing={{1}: (6, {})} | custom-call | flops 5435817984 | bytes 4718592 | tf_op jit(solution)/shard_map/part_a/pallas_call | solution.py:225
  54.5 1.1 collective-permute-start.6
  55.6 0.0 collective-permute-done.2.rest_0_
  55.6 1.4 collective-permute-start.10
  57.0 0.0 collective-permute-done.3.rest_1_
  57.0 0.0 collective-permute-done.4.rest_2_
  57.0 0.0 copy-done.3
  57.0 16.7 %cyc_captions.1.after_ref.du_ref = f32[1024,768]{1,0:T(8,128)} custom-call(f32[2]{0:T(128)S(1)} %pad_maximum_fusion.scal_ref, bf16[1024,768]{1,0:T(8,128)(2,1)S(1)} %get-tuple-element.26.hi_ref, bf16[1024,768]{1,0:T(8,128)(2,1)} %copy-done.4, f32[128,768]{1,0:T(8,128)S(1)} %collective-permute-done.2.rest_0_, f32[256,768]{1,0:T(8,128)S(1)} %collective-permute-done.3.rest_1_, ...), custom_call_target="tpu_custom_call" | custom-call | flops 9663676416 | bytes 12582912 | tf_op jit(solution)/shard_map/cyc_captions/pallas_call | solution.py:225
  73.7 0.5 collective-permute-done.1.caption_ref
  74.2 0.0 copy-start.5
  74.3 1.3 copy-done.5
  75.5 11.7 %part_b.1 = (bf16[640,1024]{1,0:T(8,128)(2,1)}, bf16[640,1024]{1,0:T(8,128)(2,1)}, bf16[640,768]{1,0:T(8,128)(2,1)S(1)}, bf16[640,768]{1,0:T(8,128)(2,1)S(1)}, f...) custom-call(f32[2]{0:T(128)S(1)} %pad_maximum_fusion.scal_ref, bf16[1024,768]{1,0:T(8,128)(2,1)} %copy-done.3, ...), custom_call_target="tpu_custom_call" | custom-call | flops 18119393280 | bytes 7864320 | tf_op jit(solution)/shard_map/part_b/pallas_call | solution.py:259
  87.2 2.1 %collective-permute-start.9 = (f32[384,768]{1,0:T(8,128)S(1)}, f32[384,768]{1,0:T(8,128)S(1)}, u32[]{:S(2)}, u32[]{:S(2)}) collective-permute-start(f32[384,768]{1,0:T(8,128)S(1)} %get-tuple-element.46), channel_id=1, source_target_pairs={{0,128},{32,160},{64,192},{96,224},{128,0},{160,32},{192,64},{224,... | collective-permute-start | bytes 3538952 | tf_op jit(solution)/shard_map/ppermute | solution.py:32
  89.4 1.4 collective-permute-start.8
  90.8 2.1 %collective-permute-start.7 = (f32[64,768]{1,0:T(8,128)S(1)}, f32[64,768]{1,0:T(8,128)S(1)}, u32[]{:S(2)}, u32[]{:S(2)}) collective-permute-start(f32[64,768]{1,0:T(8,128)S(1)} %get-tuple-element.44), channel_id=1, source_target_pairs={{0,128},{32,160},{64,192},{96,224},{128,0},{160,32},{192,64},{224,... | collective-permute-start | bytes 589832 | tf_op jit(solution)/shard_map/ppermute | solution.py:32
  92.9 0.0 copy-start.2
  92.9 1.3 copy-done.2
  94.2 8.1 %image_grad.1.after_ref = f32[1024,768]{1,0:T(8,128)} custom-call(bf16[640,1024]{1,0:T(8,128)(2,1)S(1)} %copy-done.2, bf16[640,1024]{1,0:T(8,128)(2,1)} %get-tuple-element.36.g_lo_ref, bf16[640,768]{1,0:T(8,128)(2,1)S(1)} %get-tuple-element.37.v_hi_ref, bf16[640,768]{1,0:T(8,128)(2,1)S(1)} %get-tuple-element.38.v_lo_ref, ...), custom_call_target="tpu_custom_call" | custom-call | flops 6039797760 | bytes 7864320 | tf_op jit(solution)/shard_map/image_grad/pallas_call | solution.py:274
  102.3 0.0 collective-permute-done.6.u_ref
  102.4 0.0 copy-start
  102.4 16.7 %cyc_images.1.base_ref = f32[1024,768]{1,0:T(8,128)S(1)} custom-call(f32[2]{0:T(128)S(1)} %pad_maximum_fusion.scal_ref, f32[1024,768]{1,0:T(8,128)} %collective-permute-done.6.u_ref, f32[1024,768]{1,0:T(8,128)} %caption_ref.11, f32[1024,768]{1,0:T(8,128)} %get-tuple-element.40.dv_in_ref, f32[1024,768]{1,0:T(8,128)} %image_grad.1.after_ref), custom_call_target="tpu_custom_call" | custom-call | flops 9663676416 | bytes 12582912 | tf_op jit(solution)/shard_map/cyc_images/pallas_call | solution.py:241
  119.1 0.0 copy-done
  119.1 0.2 ready.1
  119.3 0.0 collective-permute-done.10.part_ref
  119.3 1.4 %finish.3.rest_0_ = f32[1024,768]{1,0:T(8,128)} custom-call(f32[1024,768]{1,0:T(8,128)S(1)} %copy-done, f32[1024,768]{1,0:T(8,128)S(1)} %cyc_images.1.base_ref, f32[384,768]{1,0:T(8,128)S(1)} %collective-permute-done.10.part_ref), custom_call_target="tpu_custom_call" | custom-call | flops 2949120 | bytes 4718592 | tf_op jit(solution)/shard_map/finish/pallas_call | solution.py:291
  120.8 4.0 %collective-permute-done.9.part_ref = f32[384,768]{1,0:T(8,128)S(1)} collective-permute-done((f32[384,768]{1,0:T(8,128)S(1)}, f32[384,768]{1,0:T(8,128)S(1)}, u32[]{:S(2)}, u32[]{:S(2)}) %collective-permute-start.9) | collective-permute-done | bytes 1179680 | tf_op jit(solution)/shard_map/ppermute | solution.py:32
  124.8 1.4 %finish.4.rest_0_ = f32[1024,768]{1,0:T(8,128)} custom-call(f32[1024,768]{1,0:T(8,128)S(1)} %copy-done, f32[1024,768]{1,0:T(8,128)S(1)} %cyc_images.1.base_ref, f32[384,768]{1,0:T(8,128)S(1)} %collective-permute-done.9.part_ref, f32[1024,768]{1,0:T(8,128)} %finish.3.rest_0_), custom_call_target="tpu_custom_call", output_to_operand_aliasing={{}: (3, {})} | custom-call | flops 2949120 | bytes 4718592 | tf_op jit(solution)/shard_map/finish/pallas_call | solution.py:291
  126.2 11.2 %collective-permute-done.8.part_ref = f32[192,768]{1,0:T(8,128)S(1)} collective-permute-done((f32[192,768]{1,0:T(8,128)S(1)}, f32[192,768]{1,0:T(8,128)S(1)}, u32[]{:S(2)}, u32[]{:S(2)}) %collective-permute-start.8) | collective-permute-done | bytes 589856 | tf_op jit(solution)/shard_map/ppermute | solution.py:32
  137.4 1.1 finish.5.grad_in_ref
  138.6 2.0 %collective-permute-done.7.part_ref = f32[64,768]{1,0:T(8,128)S(1)} collective-permute-done((f32[64,768]{1,0:T(8,128)S(1)}, f32[64,768]{1,0:T(8,128)S(1)}, u32[]{:S(2)}, u32[]{:S(2)}) %collective-permute-start.7) | collective-permute-done | bytes 196640 | tf_op jit(solution)/shard_map/ppermute | solution.py:32
  140.5 0.8 end.1
Async XLA Ops:
  0.6 16.8 %copy-start.1 = (s32[1024]{0:T(1024)S(1)}, s32[1024]{0:T(1024)}, u32[]{:S(2)}) copy-start(s32[1024]{0:T(1024)} %param.7) | copy-start | bytes 12292
  1.7 13.6 %collective-permute-start = (f32[128,768]{1,0:T(8,128)S(1)}, f32[128,768]{1,0:T(8,128)S(1)}, u32[]{:S(2)}, u32[]{:S(2)}) collective-permute-start(f32[128,768]{1,0:T(8,128)S(1)} %slice.9), channel_id=1, source_target_pairs={{0,128},{32,160},{64,192},{96,224},{128,0},{160,32},{192,64},{224,... | collective-permute-start | bytes 1179656 | tf_op jit(solution)/shard_map/ppermute | solution.py:32
  5.1 34.8 %collective-permute-start.5 = (f32[256,768]{1,0:T(8,128)S(1)}, f32[256,768]{1,0:T(8,128)S(1)}, u32[]{:S(2)}, u32[]{:S(2)}) collective-permute-start(f32[256,768]{1,0:T(8,128)S(1)} %slice.10), channel_id=1, source_target_pairs={{0,128},{32,160},{64,192},{96,224},{128,0},{160,32},{192,64},{224,... | collective-permute-start | bytes 2359304 | tf_op jit(solution)/shard_map/ppermute | solution.py:32
  6.6 50.5 %collective-permute-start.3 = (f32[256,768]{1,0:T(8,128)S(1)}, f32[256,768]{1,0:T(8,128)S(1)}, u32[]{:S(2)}, u32[]{:S(2)}) collective-permute-start(f32[256,768]{1,0:T(8,128)S(1)} %slice.10), channel_id=1, source_target_pairs={{31,0},{0,1},{1,2},{2,3},{3,4},{4,5},{5,6},{6,7},{7,8},{8,9},{9,10... | collective-permute-start | bytes 2359304 | tf_op jit(solution)/shard_map/ppermute | solution.py:27
  6.6 49.1 %collective-permute-start.2 = (f32[128,768]{1,0:T(8,128)S(1)}, f32[128,768]{1,0:T(8,128)S(1)}, u32[]{:S(2)}, u32[]{:S(2)}) collective-permute-start(f32[128,768]{1,0:T(8,128)S(1)} %slice.9), channel_id=1, source_target_pairs={{31,0},{0,1},{1,2},{2,3},{3,4},{4,5},{5,6},{6,7},{7,8},{8,9},{9,10... | collective-permute-start | bytes 1179656 | tf_op jit(solution)/shard_map/ppermute | solution.py:27
  11.2 45.8 %collective-permute-start.4 = (f32[640,768]{1,0:T(8,128)}, f32[640,768]{1,0:T(8,128)}, u32[]{:S(2)}, u32[]{:S(2)}) collective-permute-start(f32[640,768]{1,0:T(8,128)} %slice.11), channel_id=1, source_target_pairs={{31,0},{0,1},{1,2},{2,3},{3,4},{4,5},{5,6},{6,7},{7,8},{8,9},{9,10... | collective-permute-start | bytes 5898248 | tf_op jit(solution)/shard_map/ppermute | solution.py:27
  15.3 59.0 %collective-permute-start.1 = (f32[640,768]{1,0:T(8,128)}, f32[640,768]{1,0:T(8,128)S(1)}, u32[]{:S(2)}, u32[]{:S(2)}) collective-permute-start(f32[640,768]{1,0:T(8,128)} %slice.11), channel_id=1, source_target_pairs={{0,128},{32,160},{64,192},{96,224},{128,0},{160,32},{192,64},{224,... | collective-permute-start | bytes 5898248 | tf_op jit(solution)/shard_map/ppermute | solution.py:32
  38.8 1.2 copy-start.4
  39.9 17.1 %copy-start.3 = (bf16[1024,768]{1,0:T(8,128)(2,1)}, bf16[1024,768]{1,0:T(8,128)(2,1)S(1)}, u32[]{:S(2)}) copy-start(bf16[1024,768]{1,0:T(8,128)(2,1)S(1)} %get-tuple-element.26.hi_ref) | copy-start | bytes 4718596
  54.5 47.9 %collective-permute-start.6 = (f32[1024,768]{1,0:T(8,128)}, f32[1024,768]{1,0:T(8,128)}, u32[]{:S(2)}, u32[]{:S(2)}) collective-permute-start(f32[1024,768]{1,0:T(8,128)} %get-tuple-element.39), channel_id=1, source_target_pairs={{1,0},{2,1},{3,2},{4,3},{5,4},{6,5},{7,6},{8,7},{9,8},{10,9},{11,1... | collective-permute-start | bytes 9437192 | tf_op jit(solution)/shard_map/ppermute | solution.py:27
  55.6 63.7 %collective-permute-start.10 = (f32[384,768]{1,0:T(8,128)S(1)}, f32[384,768]{1,0:T(8,128)S(1)}, u32[]{:S(2)}, u32[]{:S(2)}) collective-permute-start(f32[384,768]{1,0:T(8,128)S(1)} %get-tuple-element.47), channel_id=1, source_target_pairs={{0,128},{32,160},{64,192},{96,224},{128,0},{160,32},{192,64},{224,... | collective-permute-start | bytes 3538952 | tf_op jit(solution)/shard_map/ppermute | solution.py:32
  74.2 1.3 copy-start.5
  87.2 37.6 %collective-permute-start.9 = (f32[384,768]{1,0:T(8,128)S(1)}, f32[384,768]{1,0:T(8,128)S(1)}, u32[]{:S(2)}, u32[]{:S(2)}) collective-permute-start(f32[384,768]{1,0:T(8,128)S(1)} %get-tuple-element.46), channel_id=1, source_target_pairs={{0,128},{32,160},{64,192},{96,224},{128,0},{160,32},{192,64},{224,... | collective-permute-start | bytes 3538952 | tf_op jit(solution)/shard_map/ppermute | solution.py:32
  89.4 48.1 %collective-permute-start.8 = (f32[192,768]{1,0:T(8,128)S(1)}, f32[192,768]{1,0:T(8,128)S(1)}, u32[]{:S(2)}, u32[]{:S(2)}) collective-permute-start(f32[192,768]{1,0:T(8,128)S(1)} %get-tuple-element.45), channel_id=1, source_target_pairs={{0,128},{32,160},{64,192},{96,224},{128,0},{160,32},{192,64},{224,... | collective-permute-start | bytes 1769480 | tf_op jit(solution)/shard_map/ppermute | solution.py:32
  90.8 49.7 %collective-permute-start.7 = (f32[64,768]{1,0:T(8,128)S(1)}, f32[64,768]{1,0:T(8,128)S(1)}, u32[]{:S(2)}, u32[]{:S(2)}) collective-permute-start(f32[64,768]{1,0:T(8,128)S(1)} %get-tuple-element.44), channel_id=1, source_target_pairs={{0,128},{32,160},{64,192},{96,224},{128,0},{160,32},{192,64},{224,... | collective-permute-start | bytes 589832 | tf_op jit(solution)/shard_map/ppermute | solution.py:32
  92.9 1.3 copy-start.2
  102.4 16.7 %copy-start = (f32[1024,768]{1,0:T(8,128)S(1)}, f32[1024,768]{1,0:T(8,128)}, u32[]{:S(2)}) copy-start(f32[1024,768]{1,0:T(8,128)} %caption_ref.11) | copy-start | bytes 9437188
